TPU v7x, 32 devices: a whole 2x2x4 slice. The times are simulated.
32 devices in a mesh: band: 16 (over z, y, core), pair: 2 (over x).
Axes of the slice: x: 2, y: 2, z: 4, core: 2. Of those that a mesh axis runs over, the one named last changes fastest.
Arguments:
- frame1: bfloat16 [16, 768, 256], P('band', 'pair'), parts along dimension 1, may hold values from -6 to 6, as said below
- frame2: bfloat16 [16, 768, 256], P('band', 'pair'), parts along dimension 1, may hold values from -6 to 6, as said below
- context: bfloat16 [16, 768, 128], P('band', 'pair'), parts along dimension 1, may hold values from -6 to 6
- hidden_init: bfloat16 [16, 768, 128], P('band', 'pair'), parts along dimension 1, may hold values from -1 to 1
- offsets: int32 [2, 16, 768], P(None, 'band', 'pair'), parts along dimension 2, may hold values from -4 to 4
- w_motion: float32 [3, 128], replicated, may hold values from -3.5 to 3.5
- w_row: bfloat16 [5, 384, 384], replicated, may hold values from -0.125 to 0.125
- w_col: bfloat16 [5, 384, 384], replicated, may hold values from -0.125 to 0.125
Outputs:
- hidden: float32 [16, 768, 128], P('band', 'pair'), parts along dimension 1
- flow: float32 [2, 16, 768], P(None, 'band', 'pair'), parts along dimension 2
There are 2 independent parts, one for each index of `pair`. A program takes and returns all parts, laid end to end along the dimension named above; an argument that names none is the same for every part. Nothing has to cross between parts.
Inputs may be any that keep to these rules, and one draw needn't show every extreme that they name: `frame1`: feature vectors. `frame2`: feature vectors. offsets[0] and offsets[1] are each pixel's teacher lookup offsets, in rows and in strips.
All inputs are finite; a program needn't handle non-finite values.
Results may differ from a plain program's by a relative error of at most 0.0041.
Values may be sent and summed in bfloat16 or wider, within the bound.
A program may use at most 64 MiB of HBM per device.

v0:
```python
import math

import jax
import jax.numpy as jnp
from jax import lax
from jax.sharding import PartitionSpec as P

ITERS = 2


def passed_along(array, axis, by):
    count = lax.axis_size(axis)
    pairs = [(i, i + by) for i in range(count) if 0 <= i + by < count]
    return lax.ppermute(array, axis, pairs)


def pool_strips(frame2):
    band_rows, image_width, channels = frame2.shape
    blocks = frame2.astype(jnp.float32).reshape(band_rows, image_width // 8, 8, channels)
    return (jnp.sum(blocks, axis=2) / 2.0).astype(jnp.bfloat16)


def lookup_targets(offsets, row_first, total_rows, image_width):
    band_rows = offsets.shape[1]
    pixel_row = (
        row_first
        + jnp.arange(band_rows, dtype=jnp.int32)[:, None]
        + jnp.zeros((1, image_width), jnp.int32)
    )
    pixel_col = jnp.arange(image_width, dtype=jnp.int32)[None, :]
    target_row = pixel_row + offsets[0]
    target_col = pixel_col // 8 + offsets[1]
    inside = (
        (target_row >= 0)
        & (target_row < total_rows)
        & (target_col >= 0)
        & (target_col < image_width // 8)
    )
    target_row = jnp.where(inside, target_row, -1)
    target_col = jnp.where(inside, target_col, -1)
    return (target_row, target_col, pixel_row, pixel_col)


def strip_step(
    state, feature_rows, strip_block, row_zero, total_rows, image_width, target_row, target_col
):
    block_rows, grid_cols, channels = strip_block.shape
    scores = jnp.dot(
        feature_rows,
        strip_block.reshape(block_rows * grid_cols, channels).T,
        preferred_element_type=jnp.float32,
    ) / math.sqrt(channels)
    running_max, denominator, acc_row, acc_col, lookup = state
    new_max = jnp.maximum(running_max, jnp.max(scores, axis=1))
    shrink = jnp.exp(running_max - new_max)
    exponent = jnp.exp(scores - new_max[:, None]).reshape(-1, block_rows, grid_cols)
    strip_row = row_zero + jnp.arange(block_rows, dtype=jnp.int32)
    column_ids = jnp.arange(grid_cols, dtype=jnp.int32)
    row_centre = strip_row.astype(jnp.float32) / total_rows
    col_centre = ((8 * column_ids).astype(jnp.float32) + 3.5) / image_width
    row_weight = jnp.sum(exponent, axis=2)
    col_weight = jnp.sum(exponent, axis=1)
    scores_grid = scores.reshape(-1, block_rows, grid_cols)
    hit = (strip_row[None, :, None] == target_row[:, None, None]) & (
        column_ids[None, None, :] == target_col[:, None, None]
    )
    found = jnp.sum(jnp.where(hit, scores_grid, 0.0), axis=(1, 2))
    return (
        new_max,
        denominator * shrink + jnp.sum(row_weight, axis=1),
        acc_row * shrink + jnp.sum(row_weight * row_centre[None, :], axis=1),
        acc_col * shrink + jnp.sum(col_weight * col_centre[None, :], axis=1),
        lookup + found,
    )


def conv_valid(source, weight, conv_axis):
    out_count = source.shape[conv_axis] - 4
    summed = None
    for kernel_tap in range(5):
        tap_slice = lax.slice_in_dim(source, kernel_tap, kernel_tap + out_count, axis=conv_axis)
        tap_term = jnp.dot(
            tap_slice.reshape(-1, tap_slice.shape[-1]),
            weight[kernel_tap],
            preferred_element_type=jnp.float32,
        )
        summed = tap_term if summed is None else summed + tap_term
    out_shape = tuple(tap_slice.shape[:-1]) + (weight.shape[-1],)
    return summed.reshape(out_shape)


def pad_columns(source):
    return jnp.pad(source, ((0, 0), (2, 2), (0, 0)))


def rows_around(source, depth, mover):
    above = [
        mover(source, offset)
        for offset in list(range(depth, 0, -1)) + list(range(-1, -depth - 1, -1))
    ]
    return jnp.concatenate(above[:depth] + [source] + above[depth:], axis=0)


def row_pass(hidden, from_inputs, weight):
    width_h = hidden.shape[-1]
    hidden_half = lax.optimization_barrier(hidden.astype(jnp.bfloat16))
    gate_pair = jax.nn.sigmoid(
        conv_valid(pad_columns(hidden_half), weight[:, :width_h, : 2 * width_h], 1)
        + from_inputs[..., : 2 * width_h]
    )
    update_gate = gate_pair[..., :width_h]
    reset_gate = gate_pair[..., width_h:]
    gated = (reset_gate * hidden_half.astype(jnp.float32)).astype(jnp.bfloat16)
    candidate = jnp.tanh(
        conv_valid(pad_columns(gated), weight[:, :width_h, 2 * width_h :], 1)
        + from_inputs[..., 2 * width_h :]
    )
    return (1.0 - update_gate) * hidden + update_gate * candidate


def column_pass_each(hidden, from_inputs, weight):
    width_h = hidden.shape[-1]
    hidden_half = lax.optimization_barrier(hidden.astype(jnp.bfloat16))
    hidden_ext = rows_around(
        hidden_half, 2, lambda source, offset: passed_along(source, "band", offset)
    )
    gate_pair = jax.nn.sigmoid(
        conv_valid(hidden_ext, weight[:, :width_h, : 2 * width_h], 0)
        + from_inputs[..., : 2 * width_h]
    )
    update_gate = gate_pair[..., :width_h]
    reset_gate = gate_pair[..., width_h:]
    gated = (reset_gate * hidden_half.astype(jnp.float32)).astype(jnp.bfloat16)
    gated_ext = rows_around(gated, 2, lambda source, offset: passed_along(source, "band", offset))
    candidate = jnp.tanh(
        conv_valid(gated_ext, weight[:, :width_h, 2 * width_h :], 0)
        + from_inputs[..., 2 * width_h :]
    )
    return (1.0 - update_gate) * hidden + update_gate * candidate


def per_device(frame1, frame2, context, hidden_init, offsets, w_motion, w_row, w_col):
    band_rows, image_width, channels = frame1.shape
    total_rows = band_rows * lax.axis_size("band")
    row_first = lax.axis_index("band") * band_rows
    strips = pool_strips(frame2)
    target_row, target_col, pixel_row, pixel_col = lookup_targets(
        offsets, row_first, total_rows, image_width
    )
    pixel_count = band_rows * image_width
    features = frame1.reshape(pixel_count, channels)
    rows_target = target_row.reshape(pixel_count)
    cols_target = target_col.reshape(pixel_count)
    zeros_state = jnp.zeros((pixel_count,), jnp.float32)
    initial = (
        jnp.full((pixel_count,), -jnp.inf, jnp.float32),
        zeros_state,
        zeros_state,
        zeros_state,
        zeros_state,
    )
    state = initial
    arriving = lax.all_gather(strips, "band", axis=0, tiled=True)
    arriving_rows = arriving.shape[0]
    step_rows = min(arriving_rows, 16)
    full_steps = arriving_rows // step_rows
    blocks = arriving.reshape((full_steps, step_rows) + arriving.shape[1:])
    starts = step_rows * jnp.arange(full_steps, dtype=jnp.int32)

    def advance(carry, pieces):
        return (
            strip_step(
                carry,
                features,
                pieces[0],
                pieces[1],
                total_rows,
                image_width,
                rows_target,
                cols_target,
            ),
            None,
        )

    state, unused = lax.scan(advance, state, (blocks, starts))
    running_max, denominator, acc_row, acc_col, lookup = state
    flow_row = (acc_row / denominator).reshape(band_rows, image_width) - pixel_row.astype(
        jnp.float32
    ) / total_rows
    flow_col = (acc_col / denominator).reshape(band_rows, image_width) - pixel_col.astype(
        jnp.float32
    ) / image_width
    lookup = lookup.reshape(band_rows, image_width)
    motion = jax.nn.relu(
        flow_row[..., None] * w_motion[0]
        + flow_col[..., None] * w_motion[1]
        + lookup[..., None] * w_motion[2]
    ).astype(jnp.bfloat16)
    inputs = jnp.concatenate([context, motion], axis=-1)
    width_h = hidden_init.shape[-1]
    from_row = conv_valid(pad_columns(inputs), w_row[:, width_h:, :], 1)
    hidden = hidden_init.astype(jnp.float32)
    inputs_ext = rows_around(inputs, 2, lambda source, offset: passed_along(source, "band", offset))
    from_col = conv_valid(inputs_ext, w_col[:, width_h:, :], 0)
    for iteration in range(ITERS):
        hidden = row_pass(hidden, from_row, w_row)
        hidden = column_pass_each(hidden, from_col, w_col)
    return (hidden, jnp.stack([flow_row, flow_col]))


def solution(mesh):
    return jax.shard_map(
        per_device,
        mesh=mesh,
        in_specs=(
            P("band", "pair", None),
            P("band", "pair", None),
            P("band", "pair", None),
            P("band", "pair", None),
            P(None, "band", "pair"),
            P(),
            P(),
            P(),
        ),
        out_specs=(P("band", "pair", None), P(None, "band", "pair")),
        check_vma=False,
    )
```

profile of v0, /device:TPU:1, one launch (start us, length us, event | category | flops | bytes accessed | tf_op | source)
XLA Modules:
  0.0 116.4 jit_solution(3154691195461238958)
XLA Ops:
  2.5 24.1 %all-gather = bf16[768,256]{1,0:T(8,128)(2,1)S(1)} all-gather(bf16[48,256]{1,0:T(8,128)(2,1)S(1)} %multiply_convert_fusion), channel_id=2, replica_groups=mesh['band'=16,'pair'=2] {'band'}, dimensions={0}, use_global_device_ids=true | all-gather | bytes 417792 | tf_op jit(solution)/shard_map/all_gather | solution.py:163
  28.9 1.3 %collective-permute-start.7 = (bf16[1,384,256]{2,1,0:T(8,128)(2,1)S(1)}, bf16[1,384,256]{2,1,0:T(8,128)(2,1)S(1)}, u32[]{:S(2)}, u32[]{:S(2)}) collective-permute-start(bf16[1,384,256]{2,1,0:T(8,128)(2,1)S(1)} %pad_maximum_fusion), channel_id=1, source_target_pairs={{4,0},{6,2},{8,4},{10,6},{12,8},{14,10},{16,12},{18,14},{20,16},{2... | collective-permute-start | bytes 589832 | tf_op jit(solution)/shard_map/ppermute | solution.py:14
  30.2 4.3 %collective-permute-start.5 = (bf16[1,384,256]{2,1,0:T(8,128)(2,1)S(1)}, bf16[1,384,256]{2,1,0:T(8,128)(2,1)S(1)}, u32[]{:S(2)}, u32[]{:S(2)}) collective-permute-start(bf16[1,384,256]{2,1,0:T(8,128)(2,1)S(1)} %pad_maximum_fusion), channel_id=1, source_target_pairs={{0,2},{2,4},{4,6},{6,8},{8,10},{10,12},{12,14},{14,16},{16,18},{18... | collective-permute-start | bytes 589832 | tf_op jit(solution)/shard_map/ppermute | solution.py:14
  34.6 1.6 %collective-permute-start.4 = (bf16[1,384,256]{2,1,0:T(8,128)(2,1)S(1)}, bf16[1,384,256]{2,1,0:T(8,128)(2,1)S(1)}, u32[]{:S(2)}, u32[]{:S(2)}) collective-permute-start(bf16[1,384,256]{2,1,0:T(8,128)(2,1)S(1)} %pad_maximum_fusion), channel_id=1, source_target_pairs={{0,4},{2,6},{4,8},{6,10},{8,12},{10,14},{12,16},{14,18},{16,20},{1... | collective-permute-start | bytes 589832 | tf_op jit(solution)/shard_map/ppermute | solution.py:14
  36.2 2.7 %collective-permute-start.6 = (bf16[1,384,256]{2,1,0:T(8,128)(2,1)S(1)}, bf16[1,384,256]{2,1,0:T(8,128)(2,1)S(1)}, u32[]{:S(2)}, u32[]{:S(2)}) collective-permute-start(bf16[1,384,256]{2,1,0:T(8,128)(2,1)S(1)} %pad_maximum_fusion), channel_id=1, source_target_pairs={{2,0},{4,2},{6,4},{8,6},{10,8},{12,10},{14,12},{16,14},{18,16},{20... | collective-permute-start | bytes 589832 | tf_op jit(solution)/shard_map/ppermute | solution.py:14
  42.6 2.9 %collective-permute-start.1 = (bf16[1,384,128]{2,1,0:T(8,128)(2,1)S(1)}, bf16[1,384,128]{2,1,0:T(8,128)(2,1)S(1)}, u32[]{:S(2)}, u32[]{:S(2)}) collective-permute-start(bf16[1,384,128]{2,1,0:T(8,128)(2,1)S(1)} %get-tuple-element.49), channel_id=1, source_target_pairs={{0,2},{2,4},{4,6},{6,8},{8,10},{10,12},{12,14},{14,16},{16,18},{18... | collective-permute-start | bytes 294920 | tf_op jit(solution)/shard_map/ppermute | solution.py:14
  47.1 2.8 %collective-permute-start = (bf16[1,384,128]{2,1,0:T(8,128)(2,1)S(1)}, bf16[1,384,128]{2,1,0:T(8,128)(2,1)S(1)}, u32[]{:S(2)}, u32[]{:S(2)}) collective-permute-start(bf16[1,384,128]{2,1,0:T(8,128)(2,1)S(1)} %get-tuple-element.49), channel_id=1, source_target_pairs={{0,4},{2,6},{4,8},{6,10},{8,12},{10,14},{12,16},{14,18},{16,20},{1... | collective-permute-start | bytes 294920 | tf_op jit(solution)/shard_map/ppermute | solution.py:14
  50.1 1.4 %collective-permute-done = bf16[1,384,128]{2,1,0:T(8,128)(2,1)S(1)} collective-permute-done((bf16[1,384,128]{2,1,0:T(8,128)(2,1)S(1)}, bf16[1,384,128]{2,1,0:T(8,128)(2,1)S(1)}, u32[]{:S(2)}, u32[]{:S(2)}) %collective-permute-start) | collective-permute-done | bytes 98336 | tf_op jit(solution)/shard_map/ppermute | solution.py:14
  53.0 4.2 %collective-permute-done.3 = bf16[1,384,128]{2,1,0:T(8,128)(2,1)S(1)} collective-permute-done((bf16[1,384,128]{2,1,0:T(8,128)(2,1)S(1)}, bf16[1,384,128]{2,1,0:T(8,128)(2,1)S(1)}, u32[]{:S(2)}, u32[]{:S(2)}) %collective-permute-start.3) | collective-permute-done | bytes 98336 | tf_op jit(solution)/shard_map/ppermute | solution.py:14
  57.2 5.5 %collective-permute-start.2 = (bf16[1,384,128]{2,1,0:T(8,128)(2,1)S(1)}, bf16[1,384,128]{2,1,0:T(8,128)(2,1)S(1)}, u32[]{:S(2)}, u32[]{:S(2)}) collective-permute-start(bf16[1,384,128]{2,1,0:T(8,128)(2,1)S(1)} %get-tuple-element.49), channel_id=1, source_target_pairs={{2,0},{4,2},{6,4},{8,6},{10,8},{12,10},{14,12},{16,14},{18,16},{20... | collective-permute-start | bytes 294920 | tf_op jit(solution)/shard_map/ppermute | solution.py:14
  64.1 3.6 %collective-permute-done.2 = bf16[1,384,128]{2,1,0:T(8,128)(2,1)S(1)} collective-permute-done((bf16[1,384,128]{2,1,0:T(8,128)(2,1)S(1)}, bf16[1,384,128]{2,1,0:T(8,128)(2,1)S(1)}, u32[]{:S(2)}, u32[]{:S(2)}) %collective-permute-start.2) | collective-permute-done | bytes 98336 | tf_op jit(solution)/shard_map/ppermute | solution.py:14
  69.2 2.4 %collective-permute-start.9 = (bf16[1,384,128]{2,1,0:T(8,128)(2,1)S(1)}, bf16[1,384,128]{2,1,0:T(8,128)(2,1)S(1)}, u32[]{:S(2)}, u32[]{:S(2)}) collective-permute-start(bf16[1,384,128]{2,1,0:T(8,128)(2,1)S(1)} %fusion.57), channel_id=1, source_target_pairs={{0,2},{2,4},{4,6},{6,8},{8,10},{10,12},{12,14},{14,16},{16,18},{18... | collective-permute-start | bytes 294920 | tf_op jit(solution)/shard_map/ppermute | solution.py:14
  71.8 4.5 %collective-permute-start.8 = (bf16[1,384,128]{2,1,0:T(8,128)(2,1)S(1)}, bf16[1,384,128]{2,1,0:T(8,128)(2,1)S(1)}, u32[]{:S(2)}, u32[]{:S(2)}) collective-permute-start(bf16[1,384,128]{2,1,0:T(8,128)(2,1)S(1)} %fusion.57), channel_id=1, source_target_pairs={{0,4},{2,6},{4,8},{6,10},{8,12},{10,14},{12,16},{14,18},{16,20},{1... | collective-permute-start | bytes 294920 | tf_op jit(solution)/shard_map/ppermute | solution.py:14
  76.4 1.9 %collective-permute-start.10 = (bf16[1,384,128]{2,1,0:T(8,128)(2,1)S(1)}, bf16[1,384,128]{2,1,0:T(8,128)(2,1)S(1)}, u32[]{:S(2)}, u32[]{:S(2)}) collective-permute-start(bf16[1,384,128]{2,1,0:T(8,128)(2,1)S(1)} %fusion.57), channel_id=1, source_target_pairs={{2,0},{4,2},{6,4},{8,6},{10,8},{12,10},{14,12},{16,14},{18,16},{20... | collective-permute-start | bytes 294920 | tf_op jit(solution)/shard_map/ppermute | solution.py:14
  79.1 3.7 %collective-permute-done.10 = bf16[1,384,128]{2,1,0:T(8,128)(2,1)S(1)} collective-permute-done((bf16[1,384,128]{2,1,0:T(8,128)(2,1)S(1)}, bf16[1,384,128]{2,1,0:T(8,128)(2,1)S(1)}, u32[]{:S(2)}, u32[]{:S(2)}) %collective-permute-start.10) | collective-permute-done | bytes 98336 | tf_op jit(solution)/shard_map/ppermute | solution.py:14
  86.3 2.5 %collective-permute-start.13 = (bf16[1,384,128]{2,1,0:T(8,128)(2,1)S(1)}, bf16[1,384,128]{2,1,0:T(8,128)(2,1)S(1)}, u32[]{:S(2)}, u32[]{:S(2)}) collective-permute-start(bf16[1,384,128]{2,1,0:T(8,128)(2,1)S(1)} %get-tuple-element.53), channel_id=1, source_target_pairs={{0,2},{2,4},{4,6},{6,8},{8,10},{10,12},{12,14},{14,16},{16,18},{18... | collective-permute-start | bytes 294920 | tf_op jit(solution)/shard_map/ppermute | solution.py:14
  88.9 4.5 %collective-permute-start.12 = (bf16[1,384,128]{2,1,0:T(8,128)(2,1)S(1)}, bf16[1,384,128]{2,1,0:T(8,128)(2,1)S(1)}, u32[]{:S(2)}, u32[]{:S(2)}) collective-permute-start(bf16[1,384,128]{2,1,0:T(8,128)(2,1)S(1)} %get-tuple-element.53), channel_id=1, source_target_pairs={{0,4},{2,6},{4,8},{6,10},{8,12},{10,14},{12,16},{14,18},{16,20},{1... | collective-permute-start | bytes 294920 | tf_op jit(solution)/shard_map/ppermute | solution.py:14
  93.5 2.1 %collective-permute-start.14 = (bf16[1,384,128]{2,1,0:T(8,128)(2,1)S(1)}, bf16[1,384,128]{2,1,0:T(8,128)(2,1)S(1)}, u32[]{:S(2)}, u32[]{:S(2)}) collective-permute-start(bf16[1,384,128]{2,1,0:T(8,128)(2,1)S(1)} %get-tuple-element.53), channel_id=1, source_target_pairs={{2,0},{4,2},{6,4},{8,6},{10,8},{12,10},{14,12},{16,14},{18,16},{20... | collective-permute-start | bytes 294920 | tf_op jit(solution)/shard_map/ppermute | solution.py:14
  96.2 3.9 %collective-permute-done.14 = bf16[1,384,128]{2,1,0:T(8,128)(2,1)S(1)} collective-permute-done((bf16[1,384,128]{2,1,0:T(8,128)(2,1)S(1)}, bf16[1,384,128]{2,1,0:T(8,128)(2,1)S(1)}, u32[]{:S(2)}, u32[]{:S(2)}) %collective-permute-start.14) | collective-permute-done | bytes 98336 | tf_op jit(solution)/shard_map/ppermute | solution.py:14
  100.4 1.3 %collective-permute-start.19 = (bf16[1,384,128]{2,1,0:T(8,128)(2,1)S(1)}, bf16[1,384,128]{2,1,0:T(8,128)(2,1)S(1)}, u32[]{:S(2)}, u32[]{:S(2)}) collective-permute-start(bf16[1,384,128]{2,1,0:T(8,128)(2,1)S(1)} %fusion.55), channel_id=1, source_target_pairs={{4,0},{6,2},{8,4},{10,6},{12,8},{14,10},{16,12},{18,14},{20,16},{2... | collective-permute-start | bytes 294920 | tf_op jit(solution)/shard_map/ppermute | solution.py:14
  101.7 2.5 %collective-permute-start.17 = (bf16[1,384,128]{2,1,0:T(8,128)(2,1)S(1)}, bf16[1,384,128]{2,1,0:T(8,128)(2,1)S(1)}, u32[]{:S(2)}, u32[]{:S(2)}) collective-permute-start(bf16[1,384,128]{2,1,0:T(8,128)(2,1)S(1)} %fusion.55), channel_id=1, source_target_pairs={{0,2},{2,4},{4,6},{6,8},{8,10},{10,12},{12,14},{14,16},{16,18},{18... | collective-permute-start | bytes 294920 | tf_op jit(solution)/shard_map/ppermute | solution.py:14
  104.3 4.5 %collective-permute-start.16 = (bf16[1,384,128]{2,1,0:T(8,128)(2,1)S(1)}, bf16[1,384,128]{2,1,0:T(8,128)(2,1)S(1)}, u32[]{:S(2)}, u32[]{:S(2)}) collective-permute-start(bf16[1,384,128]{2,1,0:T(8,128)(2,1)S(1)} %fusion.55), channel_id=1, source_target_pairs={{0,4},{2,6},{4,8},{6,10},{8,12},{10,14},{12,16},{14,18},{16,20},{1... | collective-permute-start | bytes 294920 | tf_op jit(solution)/shard_map/ppermute | solution.py:14
  108.9 2.1 %collective-permute-start.18 = (bf16[1,384,128]{2,1,0:T(8,128)(2,1)S(1)}, bf16[1,384,128]{2,1,0:T(8,128)(2,1)S(1)}, u32[]{:S(2)}, u32[]{:S(2)}) collective-permute-start(bf16[1,384,128]{2,1,0:T(8,128)(2,1)S(1)} %fusion.55), channel_id=1, source_target_pairs={{2,0},{4,2},{6,4},{8,6},{10,8},{12,10},{14,12},{16,14},{18,16},{20... | collective-permute-start | bytes 294920 | tf_op jit(solution)/shard_map/ppermute | solution.py:14
  111.5 4.0 %collective-permute-done.18 = bf16[1,384,128]{2,1,0:T(8,128)(2,1)S(1)} collective-permute-done((bf16[1,384,128]{2,1,0:T(8,128)(2,1)S(1)}, bf16[1,384,128]{2,1,0:T(8,128)(2,1)S(1)}, u32[]{:S(2)}, u32[]{:S(2)}) %collective-permute-start.18) | collective-permute-done | bytes 98336 | tf_op jit(solution)/shard_map/ppermute | solution.py:14
  (103 shorter events, 20.7 us)
Async XLA Ops:
  0.6 26.8 %copy-start = (bf16[1,384,256]{2,1,0:T(8,128)(2,1)S(1)}, bf16[1,384,256]{2,1,0:T(8,128)(2,1)}, u32[]{:S(2)}) copy-start(bf16[1,384,256]{2,1,0:T(8,128)(2,1)} %param.8) | copy-start | bytes 589828
  27.9 1.0 copy-start.4
  28.3 10.5 %copy-start.3 = (bf16[5,384,384]{2,1,0:T(8,128)(2,1)S(1)}, bf16[5,384,384]{2,1,0:T(8,128)(2,1)}, u32[]{:S(2)}) copy-start(bf16[5,384,384]{2,1,0:T(8,128)(2,1)} %param.14) | copy-start | bytes 4423684
  28.9 34.6 %collective-permute-start.7 = (bf16[1,384,256]{2,1,0:T(8,128)(2,1)S(1)}, bf16[1,384,256]{2,1,0:T(8,128)(2,1)S(1)}, u32[]{:S(2)}, u32[]{:S(2)}) collective-permute-start(bf16[1,384,256]{2,1,0:T(8,128)(2,1)S(1)} %pad_maximum_fusion), channel_id=1, source_target_pairs={{4,0},{6,2},{8,4},{10,6},{12,8},{14,10},{16,12},{18,14},{20,16},{2... | collective-permute-start | bytes 589832 | tf_op jit(solution)/shard_map/ppermute | solution.py:14
  30.2 32.7 %collective-permute-start.5 = (bf16[1,384,256]{2,1,0:T(8,128)(2,1)S(1)}, bf16[1,384,256]{2,1,0:T(8,128)(2,1)S(1)}, u32[]{:S(2)}, u32[]{:S(2)}) collective-permute-start(bf16[1,384,256]{2,1,0:T(8,128)(2,1)S(1)} %pad_maximum_fusion), channel_id=1, source_target_pairs={{0,2},{2,4},{4,6},{6,8},{8,10},{10,12},{12,14},{14,16},{16,18},{18... | collective-permute-start | bytes 589832 | tf_op jit(solution)/shard_map/ppermute | solution.py:14
  34.6 28.7 %collective-permute-start.4 = (bf16[1,384,256]{2,1,0:T(8,128)(2,1)S(1)}, bf16[1,384,256]{2,1,0:T(8,128)(2,1)S(1)}, u32[]{:S(2)}, u32[]{:S(2)}) collective-permute-start(bf16[1,384,256]{2,1,0:T(8,128)(2,1)S(1)} %pad_maximum_fusion), channel_id=1, source_target_pairs={{0,4},{2,6},{4,8},{6,10},{8,12},{10,14},{12,16},{14,18},{16,20},{1... | collective-permute-start | bytes 589832 | tf_op jit(solution)/shard_map/ppermute | solution.py:14
  36.2 27.6 %collective-permute-start.6 = (bf16[1,384,256]{2,1,0:T(8,128)(2,1)S(1)}, bf16[1,384,256]{2,1,0:T(8,128)(2,1)S(1)}, u32[]{:S(2)}, u32[]{:S(2)}) collective-permute-start(bf16[1,384,256]{2,1,0:T(8,128)(2,1)S(1)} %pad_maximum_fusion), channel_id=1, source_target_pairs={{2,0},{4,2},{6,4},{8,6},{10,8},{12,10},{14,12},{16,14},{18,16},{20... | collective-permute-start | bytes 589832 | tf_op jit(solution)/shard_map/ppermute | solution.py:14
  41.7 3.8 %copy-start.2 = (bf16[5,384,384]{2,1,0:T(8,128)(2,1)S(1)}, bf16[5,384,384]{2,1,0:T(8,128)(2,1)}, u32[]{:S(2)}) copy-start(bf16[5,384,384]{2,1,0:T(8,128)(2,1)} %param.15) | copy-start | bytes 4423684
  42.6 4.5 %collective-permute-start.1 = (bf16[1,384,128]{2,1,0:T(8,128)(2,1)S(1)}, bf16[1,384,128]{2,1,0:T(8,128)(2,1)S(1)}, u32[]{:S(2)}, u32[]{:S(2)}) collective-permute-start(bf16[1,384,128]{2,1,0:T(8,128)(2,1)S(1)} %get-tuple-element.49), channel_id=1, source_target_pairs={{0,2},{2,4},{4,6},{6,8},{8,10},{10,12},{12,14},{14,16},{16,18},{18... | collective-permute-start | bytes 294920 | tf_op jit(solution)/shard_map/ppermute | solution.py:14
  47.1 4.4 %collective-permute-start = (bf16[1,384,128]{2,1,0:T(8,128)(2,1)S(1)}, bf16[1,384,128]{2,1,0:T(8,128)(2,1)S(1)}, u32[]{:S(2)}, u32[]{:S(2)}) collective-permute-start(bf16[1,384,128]{2,1,0:T(8,128)(2,1)S(1)} %get-tuple-element.49), channel_id=1, source_target_pairs={{0,4},{2,6},{4,8},{6,10},{8,12},{10,14},{12,16},{14,18},{16,20},{1... | collective-permute-start | bytes 294920 | tf_op jit(solution)/shard_map/ppermute | solution.py:14
  51.5 5.7 %collective-permute-start.3 = (bf16[1,384,128]{2,1,0:T(8,128)(2,1)S(1)}, bf16[1,384,128]{2,1,0:T(8,128)(2,1)S(1)}, u32[]{:S(2)}, u32[]{:S(2)}) collective-permute-start(bf16[1,384,128]{2,1,0:T(8,128)(2,1)S(1)} %get-tuple-element.49), channel_id=1, source_target_pairs={{4,0},{6,2},{8,4},{10,6},{12,8},{14,10},{16,12},{18,14},{20,16},{2... | collective-permute-start | bytes 294920 | tf_op jit(solution)/shard_map/ppermute | solution.py:14
  57.2 10.4 %collective-permute-start.2 = (bf16[1,384,128]{2,1,0:T(8,128)(2,1)S(1)}, bf16[1,384,128]{2,1,0:T(8,128)(2,1)S(1)}, u32[]{:S(2)}, u32[]{:S(2)}) collective-permute-start(bf16[1,384,128]{2,1,0:T(8,128)(2,1)S(1)} %get-tuple-element.49), channel_id=1, source_target_pairs={{2,0},{4,2},{6,4},{8,6},{10,8},{12,10},{14,12},{16,14},{18,16},{20... | collective-permute-start | bytes 294920 | tf_op jit(solution)/shard_map/ppermute | solution.py:14
  67.9 11.1 %collective-permute-start.11 = (bf16[1,384,128]{2,1,0:T(8,128)(2,1)S(1)}, bf16[1,384,128]{2,1,0:T(8,128)(2,1)S(1)}, u32[]{:S(2)}, u32[]{:S(2)}) collective-permute-start(bf16[1,384,128]{2,1,0:T(8,128)(2,1)S(1)} %fusion.57), channel_id=1, source_target_pairs={{4,0},{6,2},{8,4},{10,6},{12,8},{14,10},{16,12},{18,14},{20,16},{2... | collective-permute-start | bytes 294920 | tf_op jit(solution)/shard_map/ppermute | solution.py:14
  69.2 9.1 %collective-permute-start.9 = (bf16[1,384,128]{2,1,0:T(8,128)(2,1)S(1)}, bf16[1,384,128]{2,1,0:T(8,128)(2,1)S(1)}, u32[]{:S(2)}, u32[]{:S(2)}) collective-permute-start(bf16[1,384,128]{2,1,0:T(8,128)(2,1)S(1)} %fusion.57), channel_id=1, source_target_pairs={{0,2},{2,4},{4,6},{6,8},{8,10},{10,12},{12,14},{14,16},{16,18},{18... | collective-permute-start | bytes 294920 | tf_op jit(solution)/shard_map/ppermute | solution.py:14
  71.8 7.0 %collective-permute-start.8 = (bf16[1,384,128]{2,1,0:T(8,128)(2,1)S(1)}, bf16[1,384,128]{2,1,0:T(8,128)(2,1)S(1)}, u32[]{:S(2)}, u32[]{:S(2)}) collective-permute-start(bf16[1,384,128]{2,1,0:T(8,128)(2,1)S(1)} %fusion.57), channel_id=1, source_target_pairs={{0,4},{2,6},{4,8},{6,10},{8,12},{10,14},{12,16},{14,18},{16,20},{1... | collective-permute-start | bytes 294920 | tf_op jit(solution)/shard_map/ppermute | solution.py:14
  76.4 6.4 %collective-permute-start.10 = (bf16[1,384,128]{2,1,0:T(8,128)(2,1)S(1)}, bf16[1,384,128]{2,1,0:T(8,128)(2,1)S(1)}, u32[]{:S(2)}, u32[]{:S(2)}) collective-permute-start(bf16[1,384,128]{2,1,0:T(8,128)(2,1)S(1)} %fusion.57), channel_id=1, source_target_pairs={{2,0},{4,2},{6,4},{8,6},{10,8},{12,10},{14,12},{16,14},{18,16},{20... | collective-permute-start | bytes 294920 | tf_op jit(solution)/shard_map/ppermute | solution.py:14
  85.0 11.0 %collective-permute-start.15 = (bf16[1,384,128]{2,1,0:T(8,128)(2,1)S(1)}, bf16[1,384,128]{2,1,0:T(8,128)(2,1)S(1)}, u32[]{:S(2)}, u32[]{:S(2)}) collective-permute-start(bf16[1,384,128]{2,1,0:T(8,128)(2,1)S(1)} %get-tuple-element.53), channel_id=1, source_target_pairs={{4,0},{6,2},{8,4},{10,6},{12,8},{14,10},{16,12},{18,14},{20,16},{2... | collective-permute-start | bytes 294920 | tf_op jit(solution)/shard_map/ppermute | solution.py:14
  86.3 9.3 %collective-permute-start.13 = (bf16[1,384,128]{2,1,0:T(8,128)(2,1)S(1)}, bf16[1,384,128]{2,1,0:T(8,128)(2,1)S(1)}, u32[]{:S(2)}, u32[]{:S(2)}) collective-permute-start(bf16[1,384,128]{2,1,0:T(8,128)(2,1)S(1)} %get-tuple-element.53), channel_id=1, source_target_pairs={{0,2},{2,4},{4,6},{6,8},{8,10},{10,12},{12,14},{14,16},{16,18},{18... | collective-permute-start | bytes 294920 | tf_op jit(solution)/shard_map/ppermute | solution.py:14
  88.9 6.9 %collective-permute-start.12 = (bf16[1,384,128]{2,1,0:T(8,128)(2,1)S(1)}, bf16[1,384,128]{2,1,0:T(8,128)(2,1)S(1)}, u32[]{:S(2)}, u32[]{:S(2)}) collective-permute-start(bf16[1,384,128]{2,1,0:T(8,128)(2,1)S(1)} %get-tuple-element.53), channel_id=1, source_target_pairs={{0,4},{2,6},{4,8},{6,10},{8,12},{10,14},{12,16},{14,18},{16,20},{1... | collective-permute-start | bytes 294920 | tf_op jit(solution)/shard_map/ppermute | solution.py:14
  93.5 6.7 %collective-permute-start.14 = (bf16[1,384,128]{2,1,0:T(8,128)(2,1)S(1)}, bf16[1,384,128]{2,1,0:T(8,128)(2,1)S(1)}, u32[]{:S(2)}, u32[]{:S(2)}) collective-permute-start(bf16[1,384,128]{2,1,0:T(8,128)(2,1)S(1)} %get-tuple-element.53), channel_id=1, source_target_pairs={{2,0},{4,2},{6,4},{8,6},{10,8},{12,10},{14,12},{16,14},{18,16},{20... | collective-permute-start | bytes 294920 | tf_op jit(solution)/shard_map/ppermute | solution.py:14
  100.4 11.0 %collective-permute-start.19 = (bf16[1,384,128]{2,1,0:T(8,128)(2,1)S(1)}, bf16[1,384,128]{2,1,0:T(8,128)(2,1)S(1)}, u32[]{:S(2)}, u32[]{:S(2)}) collective-permute-start(bf16[1,384,128]{2,1,0:T(8,128)(2,1)S(1)} %fusion.55), channel_id=1, source_target_pairs={{4,0},{6,2},{8,4},{10,6},{12,8},{14,10},{16,12},{18,14},{20,16},{2... | collective-permute-start | bytes 294920 | tf_op jit(solution)/shard_map/ppermute | solution.py:14
  101.7 9.3 %collective-permute-start.17 = (bf16[1,384,128]{2,1,0:T(8,128)(2,1)S(1)}, bf16[1,384,128]{2,1,0:T(8,128)(2,1)S(1)}, u32[]{:S(2)}, u32[]{:S(2)}) collective-permute-start(bf16[1,384,128]{2,1,0:T(8,128)(2,1)S(1)} %fusion.55), channel_id=1, source_target_pairs={{0,2},{2,4},{4,6},{6,8},{8,10},{10,12},{12,14},{14,16},{16,18},{18... | collective-permute-start | bytes 294920 | tf_op jit(solution)/shard_map/ppermute | solution.py:14
  104.3 6.8 %collective-permute-start.16 = (bf16[1,384,128]{2,1,0:T(8,128)(2,1)S(1)}, bf16[1,384,128]{2,1,0:T(8,128)(2,1)S(1)}, u32[]{:S(2)}, u32[]{:S(2)}) collective-permute-start(bf16[1,384,128]{2,1,0:T(8,128)(2,1)S(1)} %fusion.55), channel_id=1, source_target_pairs={{0,4},{2,6},{4,8},{6,10},{8,12},{10,14},{12,16},{14,18},{16,20},{1... | collective-permute-start | bytes 294920 | tf_op jit(solution)/shard_map/ppermute | solution.py:14
  108.9 6.7 %collective-permute-start.18 = (bf16[1,384,128]{2,1,0:T(8,128)(2,1)S(1)}, bf16[1,384,128]{2,1,0:T(8,128)(2,1)S(1)}, u32[]{:S(2)}, u32[]{:S(2)}) collective-permute-start(bf16[1,384,128]{2,1,0:T(8,128)(2,1)S(1)} %fusion.55), channel_id=1, source_target_pairs={{2,0},{4,2},{6,4},{8,6},{10,8},{12,10},{14,12},{16,14},{18,16},{20... | collective-permute-start | bytes 294920 | tf_op jit(solution)/shard_map/ppermute | solution.py:14
  (1 other events, 0.9 us)
where the time goes:
time: 117 us; the launch traced here: 116 us
  starting transfers between devices  53.4 us (46%)
  blocking collectives  24.1 us (21%)
  waiting for transfers between devices  21.7 us (19%)
  matrix products  11.1 us (9%)
  other arithmetic  3.59 us (3%)
  between operations  1.34 us (1%)
  local copies, waits for them, and re-layouts  1.17 us (1%)
    ppermute x20, starting transfers between devices, passed_along(): return lax.ppermute(array, axis, pairs)  53.4 us
    all_gather x1, blocking collectives, per_device(): arriving = lax.all_gather(strips, 'band', axis=0, tiled=True)  24.1 us
    ppermute x20, waiting for transfers between devices, passed_along(): return lax.ppermute(array, axis, pairs)  21.7 us
    dot_general x50, matrix products, conv_valid(): jnp.dot(tap_slice.reshape(-1, tap_slice.shape[-1]), weight[kernel_tap], p...  10.7 us
  transfers between devices with their start and end apart: 20, of which 8 were waited for; matrix products, arithmetic and copies ran while one was open for 7% of the time, Pallas kernels for 0%

commit v1 on v0

--- a/solution.py
+++ b/solution.py
@@ -1,8 +1,11 @@
+import functools
 import math
 
 import jax
 import jax.numpy as jnp
 from jax import lax
+from jax.experimental import pallas as pl
+from jax.experimental.pallas import tpu as pltpu
 from jax.sharding import PartitionSpec as P
 
 ITERS = 2
@@ -139,7 +142,7 @@
     return (1.0 - update_gate) * hidden + update_gate * candidate
 
 
-def per_device(frame1, frame2, context, hidden_init, offsets, w_motion, w_row, w_col):
+def per_device_rows(frame1, frame2, context, hidden_init, offsets, w_motion, w_row, w_col):
     band_rows, image_width, channels = frame1.shape
     total_rows = band_rows * lax.axis_size("band")
     row_first = lax.axis_index("band") * band_rows
@@ -208,7 +211,456 @@
     return (hidden, jnp.stack([flow_row, flow_col]))
 
 
+BF = jnp.bfloat16
+F32 = jnp.float32
+MESH = pl.DeviceIdType.MESH
+HALO = 4
+
+
+def mm(a, b):
+    return jnp.dot(a, b, preferred_element_type=F32)
+
+
+def shifted_taps(padded, count):
+    return jnp.concatenate(
+        [padded[6 + k : 6 + k + count, :].astype(BF) for k in range(5)], axis=1
+    )
+
+
+def row_taps(value, step):
+    zeros = jnp.zeros((2 * step, value.shape[1]), value.dtype)
+    tall = jnp.concatenate([zeros, value, zeros], axis=0)
+    count = value.shape[0]
+    return jnp.concatenate([tall[k * step : k * step + count] for k in range(5)], axis=1)
+
+
+def tap_weights(w_ref, first, low, high):
+    return w_ref[:, first : first + 128, low:high].reshape(5 * 128, high - low)
+
+
+def fused_kernel(
+    bands,
+    frame1,
+    frame2,
+    context,
+    hidden_init,
+    offsets,
+    w_motion,
+    w_row_hbm,
+    w_col_hbm,
+    hidden_out,
+    flow_out,
+    w_row,
+    w_col,
+    strips,
+    scores,
+    ctx_stage,
+    ctx_recv,
+    flow_stage,
+    flow_recv,
+    hid_stage,
+    hid_recv,
+    out_stage,
+    out_recv,
+    pad_ctx,
+    pad_hid,
+    pad_mot,
+    pad_gate,
+    win_ctx,
+    win_mot,
+    win_hid,
+    win_gate,
+    acc_row,
+    gate_row,
+    acc_col,
+    acc_row2,
+    w_sem,
+    strip_send,
+    strip_recv,
+    ctx_ssem,
+    ctx_rsem,
+    flow_ssem,
+    flow_rsem,
+    hid_ssem,
+    hid_rsem,
+    out_ssem,
+    out_rsem,
+):
+    width = frame1.shape[0]
+    own = width // bands
+    win = own + 2 * HALO
+    grid_cols = width // 8
+    me = lax.axis_index("band")
+    pair = lax.axis_index("pair")
+
+    copy_row = pltpu.make_async_copy(w_row_hbm, w_row, w_sem.at[0])
+    copy_col = pltpu.make_async_copy(w_col_hbm, w_col, w_sem.at[1])
+    copy_row.start()
+    copy_col.start()
+
+    barrier = pltpu.get_barrier_semaphore()
+
+    def greet(k, carry):
+        pl.semaphore_signal(
+            barrier, inc=1, device_id=(lax.rem(me + k, bands), pair), device_id_type=MESH
+        )
+        return carry
+
+    lax.fori_loop(1, bands, greet, 0)
+
+    blocks = frame2[...].astype(F32).reshape(grid_cols, 8, frame2.shape[1])
+    strips[pl.ds(me, 1)] = (jnp.sum(blocks, axis=1) / 2.0).astype(BF)[None]
+
+    def zero_ends(ref, count):
+        ref[0:8, :] = jnp.zeros((8, 128), F32)
+        ref[8 + count : 16 + count, :] = jnp.zeros((8, 128), F32)
+
+    for ref in (pad_ctx, pad_hid, pad_mot, pad_gate):
+        zero_ends(ref, width)
+    for ref in (win_ctx, win_mot, win_hid, win_gate):
+        zero_ends(ref, bands * win)
+
+    pad_ctx[8 : 8 + width, :] = context[...].astype(F32)
+    pad_hid[8 : 8 + width, :] = hidden_init[...].astype(F32)
+
+    def stage_windows(stage, padded):
+        for d in range(bands):
+            first = 8 + own * d - HALO
+            stage[d] = padded[first : first + win, :].astype(BF)
+
+    stage_windows(ctx_stage, pad_ctx)
+
+    def send(stage, recv, ssem, rsem, to):
+        return pltpu.make_async_remote_copy(
+            src_ref=stage.at[to],
+            dst_ref=recv.at[me],
+            send_sem=ssem.at[to],
+            recv_sem=rsem.at[me],
+            device_id=(to, pair),
+            device_id_type=MESH,
+        )
+
+    def scatter(stage, recv, ssem, rsem):
+        def one(k, carry):
+            send(stage, recv, ssem, rsem, lax.rem(me + k, bands)).start()
+            return carry
+
+        lax.fori_loop(1, bands, one, 0)
+        recv[pl.ds(me, 1)] = stage[pl.ds(me, 1)]
+
+    def collect(stage, recv, ssem, rsem):
+        def one(k, carry):
+            source = lax.rem(me + bands - k, bands)
+            pltpu.make_async_remote_copy(
+                src_ref=stage.at[source],
+                dst_ref=recv.at[source],
+                send_sem=ssem.at[source],
+                recv_sem=rsem.at[source],
+                device_id=(source, pair),
+                device_id_type=MESH,
+            ).wait_recv()
+            return carry
+
+        lax.fori_loop(1, bands, one, 0)
+
+    def sent(stage, recv, ssem, rsem):
+        def one(k, carry):
+            send(stage, recv, ssem, rsem, lax.rem(me + k, bands)).wait_send()
+            return carry
+
+        lax.fori_loop(1, bands, one, 0)
+
+    pl.semaphore_wait(barrier, bands - 1)
+
+    level = me // 4
+    place = lax.rem(me, 4)
+    core = lax.rem(me, 2)
+    sibling = me + 1 - 2 * core
+    across = me + 2 - 4 * lax.rem(me // 2, 2)
+    levels = (
+        level,
+        level + 1 - 2 * lax.rem(level, 2),
+        2 - level // 2,
+        3 - 3 * (level // 2),
+    )
+    line = [4 * other + place for other in levels]
+    across_line = [4 * other + (across - 4 * level) for other in levels]
+    started = []
+
+    def pass_on(block, to, slot):
+        copy = pltpu.make_async_remote_copy(
+            src_ref=strips.at[block],
+            dst_ref=strips.at[block],
+            send_sem=strip_send.at[slot],
+            recv_sem=strip_recv.at[block],
+            device_id=(to, pair),
+            device_id_type=MESH,
+        )
+        copy.start()
+        started.append(copy)
+
+    def arrived(block):
+        pltpu.make_async_remote_copy(
+            src_ref=strips.at[block],
+            dst_ref=strips.at[block],
+            send_sem=strip_send.at[0],
+            recv_sem=strip_recv.at[block],
+            device_id=(sibling, pair),
+            device_id_type=MESH,
+        ).wait_recv()
+
+    pass_on(me, line[1], 0)
+    pass_on(me, across, 1)
+    pass_on(me, line[2], 2)
+    pass_on(me, line[3], 3)
+    pass_on(me, sibling, 4)
+
+    copy_row.wait()
+    gate_row[...] = mm(shifted_taps(pad_hid, width), tap_weights(w_row, 0, 0, 256))
+
+    for i in (1, 2, 3):
+        arrived(line[i])
+        pass_on(line[i], across, 4 + i)
+        pass_on(line[i], sibling, 7 + i)
+    scatter(ctx_stage, ctx_recv, ctx_ssem, ctx_rsem)
+    acc_row[...] = mm(shifted_taps(pad_ctx, width), tap_weights(w_row, 128, 0, 384))
+    for i in (0, 1, 2, 3):
+        arrived(across_line[i])
+        pass_on(across_line[i], sibling, 11 + i)
+    for i in (0, 1, 2, 3):
+        arrived(line[i] + 1 - 2 * core)
+    for i in (0, 1, 2, 3):
+        arrived(across_line[i] + 1 - 2 * core)
+
+    scores[...] = lax.dot_general(
+        strips[...].reshape(bands * grid_cols, frame1.shape[1]),
+        frame1[...],
+        (((1,), (1,)), ((), ())),
+        preferred_element_type=F32,
+    ) * (1.0 / math.sqrt(frame1.shape[1]))
+
+    row_f = me.astype(F32) / bands
+    parts = []
+    strip_ids = lax.broadcasted_iota(jnp.int32, (grid_cols, 128), 0)
+    centres = ((8 * strip_ids).astype(F32) + 3.5) / width
+    for lanes in range(0, width, 128):
+        cut = slice(lanes, lanes + 128)
+        column = lanes + lax.broadcasted_iota(jnp.int32, (1, 128), 1)
+        target_row = me + offsets[0, :, cut]
+        target_col = column // 8 + offsets[1, :, cut]
+        inside = (
+            (target_row >= 0)
+            & (target_row < bands)
+            & (target_col >= 0)
+            & (target_col < grid_cols)
+        )
+        target = jnp.where(inside, target_row * grid_cols + target_col, -1)
+        highest = scores[0:grid_cols, cut]
+        for r in range(1, bands):
+            highest = jnp.maximum(highest, scores[r * grid_cols : (r + 1) * grid_cols, cut])
+        highest = jnp.max(highest, axis=0, keepdims=True)
+        by_col = jnp.zeros((grid_cols, 128), F32)
+        by_row = jnp.zeros((8, 128), F32)
+        found = jnp.zeros((grid_cols, 128), F32)
+        for r in range(bands):
+            block = scores[r * grid_cols : (r + 1) * grid_cols, cut]
+            raised = jnp.exp(block - highest)
+            by_col = by_col + raised
+            if r:
+                folded = jnp.sum(raised.reshape(grid_cols // 8, 8, 128), axis=0)
+                by_row = by_row + folded * (r / bands)
+            found = found + jnp.where(strip_ids + r * grid_cols == target, block, 0.0)
+        total = jnp.sum(by_col, axis=0, keepdims=True)
+        moved_row = jnp.sum(by_row, axis=0, keepdims=True) / total
+        moved_col = jnp.sum(by_col * centres, axis=0, keepdims=True) / total
+        flow_row = moved_row - row_f
+        flow_col = moved_col - column.astype(F32) / width
+        flow_out[0, :, cut] = flow_row
+        flow_out[1, :, cut] = flow_col
+        parts.append(
+            jnp.concatenate(
+                [
+                    flow_row,
+                    flow_col,
+                    jnp.sum(found, axis=0, keepdims=True),
+                    jnp.zeros((5, 128), F32),
+                ],
+                axis=0,
+            )
+        )
+
+    three = jnp.concatenate(parts + [jnp.zeros((8, 128), F32)], axis=1)
+    span = width + 128
+    line_id = lax.broadcasted_iota(jnp.int32, (8, span), 0)
+    spread = jnp.where(line_id == 1, pltpu.roll(three, 32, 1), three)
+    spread = jnp.where(line_id == 2, pltpu.roll(three, 64, 1), spread)
+    lane_group = lax.broadcasted_iota(jnp.int32, (8, 128), 1) // 32
+    wanted = lane_group == lax.broadcasted_iota(jnp.int32, (8, 128), 0)
+    for d in range(bands):
+        turned = pltpu.roll(spread, (span - (own * d - HALO)) % span, 1)[:, 0:128]
+        flow_stage[d] = jnp.sum(jnp.where(wanted, turned, 0.0), axis=0, keepdims=True)
+    scatter(flow_stage, flow_recv, flow_ssem, flow_rsem)
+
+    def motion_of(first, second, third):
+        return jnp.maximum(
+            first * w_motion[0:1, :] + second * w_motion[1:2, :] + third * w_motion[2:3, :],
+            0.0,
+        )
+
+    for i, part in enumerate(parts):
+        upright = jnp.concatenate([part, jnp.zeros((120, 128), F32)], axis=0).T
+        pad_mot[8 + 128 * i : 136 + 128 * i, :] = motion_of(
+            upright[:, 0:1], upright[:, 1:2], upright[:, 2:3]
+        )
+    acc = mm(shifted_taps(pad_mot, width), tap_weights(w_row, 256, 0, 384)) + acc_row[...]
+    start = pad_hid[8 : 8 + width, :]
+    update = jax.nn.sigmoid(gate_row[:, 0:128] + acc[:, 0:128])
+    reset = jax.nn.sigmoid(gate_row[:, 128:256] + acc[:, 128:256])
+    pad_gate[8 : 8 + width, :] = reset * start
+    candidate = jnp.tanh(
+        mm(shifted_taps(pad_gate, width), tap_weights(w_row, 0, 256, 384)) + acc[:, 256:384]
+    )
+    pad_hid[8 : 8 + width, :] = (1.0 - update) * start + update * candidate
+    stage_windows(hid_stage, pad_hid)
+    scatter(hid_stage, hid_recv, hid_ssem, hid_rsem)
+
+    pixels = bands * win
+    collect(ctx_stage, ctx_recv, ctx_ssem, ctx_rsem)
+    copy_col.wait()
+    ctx = ctx_recv[...].reshape(pixels, 128)
+    win_ctx[8 : 8 + pixels, :] = ctx.astype(F32)
+    acc_col[...] = mm(row_taps(ctx, win), tap_weights(w_col, 128, 0, 384))
+    acc_row2[...] = mm(shifted_taps(win_ctx, pixels), tap_weights(w_row, 128, 0, 384))
+    collect(flow_stage, flow_recv, flow_ssem, flow_rsem)
+    upright = jnp.concatenate(
+        [flow_recv[r] for r in range(bands)] + [jnp.zeros((128 - bands, 128), F32)], axis=0
+    ).T
+    for r in range(bands):
+        win_mot[8 + win * r : 8 + win * (r + 1), :] = motion_of(
+            upright[0:win, r : r + 1],
+            upright[win : 2 * win, r : r + 1],
+            upright[2 * win : 3 * win, r : r + 1],
+        )
+    motion = win_mot[8 : 8 + pixels, :].astype(BF)
+    acc_col[...] += mm(row_taps(motion, win), tap_weights(w_col, 256, 0, 384))
+    acc_row2[...] += mm(shifted_taps(win_mot, pixels), tap_weights(w_row, 256, 0, 384))
+
+    collect(hid_stage, hid_recv, hid_ssem, hid_rsem)
+    state_half = hid_recv[...].reshape(pixels, 128)
+    state = state_half.astype(F32)
+
+    def gru(state, half, acc, weight, taps_of):
+        pre = mm(taps_of(half, win_hid), tap_weights(weight, 0, 0, 256)) + acc[:, 0:256]
+        update = jax.nn.sigmoid(pre[:, 0:128])
+        reset = jax.nn.sigmoid(pre[:, 128:256])
+        gated = (reset * half.astype(F32)).astype(BF)
+        candidate = jnp.tanh(
+            mm(taps_of(gated, win_gate), tap_weights(weight, 0, 256, 384)) + acc[:, 256:384]
+        )
+        return (1.0 - update) * state + update * candidate
+
+    def taps_down(value, unused):
+        return row_taps(value, win)
+
+    def taps_along(value, padded):
+        padded[8 : 8 + pixels, :] = value.astype(F32)
+        return shifted_taps(padded, pixels)
+
+    state = gru(state, state_half, acc_col, w_col, taps_down)
+    state = gru(state, state.astype(BF), acc_row2, w_row, taps_along)
+    state = gru(state, state.astype(BF), acc_col, w_col, taps_down)
+    win_hid[8 : 8 + pixels, :] = state
+    for r in range(bands):
+        first = 8 + win * r + HALO
+        out_stage[r] = win_hid[first : first + own, :].astype(BF)
+    scatter(out_stage, out_recv, out_ssem, out_rsem)
+    for copy in started:
+        copy.wait_send()
+    sent(ctx_stage, ctx_recv, ctx_ssem, ctx_rsem)
+    sent(flow_stage, flow_recv, flow_ssem, flow_rsem)
+    sent(hid_stage, hid_recv, hid_ssem, hid_rsem)
+    collect(out_stage, out_recv, out_ssem, out_rsem)
+    hidden_out[...] = out_recv[...]
+    sent(out_stage, out_recv, out_ssem, out_rsem)
+
+
+def per_device_columns(
+    bands, frame1, frame2, context, hidden_init, offsets, w_motion, w_row, w_col
+):
+    unused, width, channels = frame1.shape
+    own = width // bands
+    win = own + 2 * HALO
+    pixels = bands * win
+    vmem = pl.BlockSpec(memory_space=pltpu.VMEM)
+    hbm = pl.BlockSpec(memory_space=pl.ANY)
+    dma = pltpu.SemaphoreType.DMA
+    tall = pltpu.VMEM((width + 16, 128), F32)
+    wide = pltpu.VMEM((pixels + 16, 128), F32)
+    hidden, flow = pl.pallas_call(
+        functools.partial(fused_kernel, bands),
+        out_shape=(
+            jax.ShapeDtypeStruct((bands, own, 128), BF),
+            jax.ShapeDtypeStruct((2, 1, width), F32),
+        ),
+        in_specs=[vmem] * 6 + [hbm] * 2,
+        out_specs=(vmem, vmem),
+        scratch_shapes=[
+            pltpu.VMEM(w_row.shape, BF),
+            pltpu.VMEM(w_col.shape, BF),
+            pltpu.VMEM((bands, width // 8, channels), BF),
+            pltpu.VMEM((bands * width // 8, width), F32),
+            pltpu.VMEM((bands, win, 128), BF),
+            pltpu.VMEM((bands, win, 128), BF),
+            pltpu.VMEM((bands, 1, 128), F32),
+            pltpu.VMEM((bands, 1, 128), F32),
+            pltpu.VMEM((bands, win, 128), BF),
+            pltpu.VMEM((bands, win, 128), BF),
+            pltpu.VMEM((bands, own, 128), BF),
+            pltpu.VMEM((bands, own, 128), BF),
+            tall,
+            tall,
+            tall,
+            tall,
+            wide,
+            wide,
+            wide,
+            wide,
+            pltpu.VMEM((width, 384), F32),
+            pltpu.VMEM((width, 256), F32),
+            pltpu.VMEM((pixels, 384), F32),
+            pltpu.VMEM((pixels, 384), F32),
+            dma((2,)),
+            dma((15,)),
+        ]
+        + [dma((bands,))] * 9,
+        compiler_params=pltpu.CompilerParams(
+            collective_id=0, has_side_effects=True, vmem_limit_bytes=48 * 1024 * 1024
+        ),
+        cost_estimate=pl.CostEstimate(
+            flops=2_400_000_000, bytes_accessed=4_500_000, transcendentals=700_000
+        ),
+    )(
+        frame1.reshape(width, channels),
+        frame2.reshape(width, channels),
+        context.reshape(width, 128),
+        hidden_init.reshape(width, 128),
+        offsets,
+        w_motion,
+        w_row,
+        w_col,
+    )
+    return (hidden.astype(F32).reshape(1, width, 128), flow)
+
+
 def solution(mesh):
+    bands = mesh.shape["band"]
+
+    def per_device(frame1, frame2, *rest):
+        own = frame1.shape[1] // bands
+        if bands == 16 and frame1.shape[0] == 1 and own + 2 * HALO == 32:
+            return per_device_columns(bands, frame1, frame2, *rest)
+        return per_device_rows(frame1, frame2, *rest)
+
     return jax.shard_map(
         per_device,
         mesh=mesh,

time: 117 us -> 40 us (0.34)
  the two profiles are of different devices: /device:TPU:1 before, /device:TPU:0 now
where the time goes in v1:
time: 40 us; the launch traced here: 39.6 us
  Pallas kernels  30 us (75%)
  local copies, waits for them, and re-layouts  8.32 us (21%)
  other arithmetic  0.69 us (2%)
  between operations  0.66 us (2%)
    pallas_call x1, Pallas kernels, per_device_columns(): pl.pallas_call(functools.partial(fused_kernel, bands), out_shape=(jax.Sha...  30 us
    unnamed x17, local copies, waits for them, and re-layouts  8.32 us

profile of v1, /device:TPU:0, one launch (start us, length us, event | category | flops | bytes accessed | tf_op | source)
XLA Modules:
  0.0 39.6 jit_solution(3584121664361466705)
XLA Ops:
  0.6 0.0 copy-start
  0.6 1.4 %copy-done = bf16[5,384,384]{2,1,0:T(8,128)(2,1)S(1)} copy-done((bf16[5,384,384]{2,1,0:T(8,128)(2,1)S(1)}, bf16[5,384,384]{2,1,0:T(8,128)(2,1)}, u32[]{:S(2)}) %copy-start) | copy-done | bytes 1474584
  2.0 0.0 copy-start.1
  2.0 1.4 %copy-done.1 = bf16[5,384,384]{2,1,0:T(8,128)(2,1)S(1)} copy-done((bf16[5,384,384]{2,1,0:T(8,128)(2,1)S(1)}, bf16[5,384,384]{2,1,0:T(8,128)(2,1)}, u32[]{:S(2)}) %copy-start.1) | copy-done | bytes 1474584
  3.4 0.0 copy-start.2
  3.4 0.9 %copy-done.2 = bf16[1,384,256]{2,1,0:T(8,128)(2,1)S(1)} copy-done((bf16[1,384,256]{2,1,0:T(8,128)(2,1)S(1)}, bf16[1,384,256]{2,1,0:T(8,128)(2,1)}, u32[]{:S(2)}) %copy-start.2) | copy-done | bytes 196632
  4.3 0.0 copy-start.3
  4.3 0.9 %copy-done.3 = bf16[1,384,256]{2,1,0:T(8,128)(2,1)S(1)} copy-done((bf16[1,384,256]{2,1,0:T(8,128)(2,1)S(1)}, bf16[1,384,256]{2,1,0:T(8,128)(2,1)}, u32[]{:S(2)}) %copy-start.3) | copy-done | bytes 196632
  5.2 0.0 copy-start.4
  5.2 0.9 %copy-done.4 = bf16[1,384,128]{2,1,0:T(8,128)(2,1)S(1)} copy-done((bf16[1,384,128]{2,1,0:T(8,128)(2,1)S(1)}, bf16[1,384,128]{2,1,0:T(8,128)(2,1)}, u32[]{:S(2)}) %copy-start.4) | copy-done | bytes 98328
  6.1 0.0 copy-start.5
  6.1 0.9 %copy-done.5 = bf16[1,384,128]{2,1,0:T(8,128)(2,1)S(1)} copy-done((bf16[1,384,128]{2,1,0:T(8,128)(2,1)S(1)}, bf16[1,384,128]{2,1,0:T(8,128)(2,1)}, u32[]{:S(2)}) %copy-start.5) | copy-done | bytes 98328
  7.0 0.0 copy-start.6
  7.0 0.7 %copy-done.6 = s32[2,1,384]{2,1,0:T(1,128)S(1)} copy-done((s32[2,1,384]{2,1,0:T(1,128)S(1)}, s32[2,1,384]{2,1,0:T(1,128)}, u32[]{:S(2)}) %copy-start.6) | copy-done | bytes 3096
  7.7 0.0 copy-start.7
  7.7 0.7 %copy-done.7 = f32[3,128]{1,0:T(4,128)S(1)} copy-done((f32[3,128]{1,0:T(4,128)S(1)}, f32[3,128]{1,0:T(4,128)}, u32[]{:S(2)}) %copy-start.7) | copy-done | bytes 1560
  8.4 30.0 %shard_map.95 = (bf16[16,24,128]{2,1,0:T(8,128)(2,1)S(1)}, f32[2,1,384]{2,1,0:T(1,128)S(1)}) custom-call(bf16[384,256]{1,0:T(8,128)(2,1)S(1)} %bitcast.9, bf16[384,256]{1,0:T(8,128)(2,1)S(1)} %bitcast.10, bf16[384,128]{1,0:T(8,128)(2,1)S(1)} %bitcast.11, bf16[384,128]{1,0:T(8,128)(2,1)S(1)} %bitcast.12, s32[2,1,384]{2,1,0:T(1,128)S(1)} %copy-done.6, ...), custom_call_target="tpu_custom_call" | custom-call | flops 2400000000 | bytes 4500000 | tf_op jit(solution)/shard_map/pallas_call | solution.py:599
  38.4 0.7 %bitcast_convert_fusion = f32[1,384,128]{2,1,0:T(8,128)} fusion(bf16[1,384,128]{2,1,0:T(8,128)(2,1)S(1)} %bitcast.8), kind=kLoop, calls=%fused_computation | loop fusion | flops 49152 | bytes 294912 | tf_op jit(solution)/shard_map/reshape | solution.py:652
  39.0 0.6 %copy.11 = f32[2,1,384]{2,1,0:T(1,128)} copy(f32[2,1,384]{2,1,0:T(1,128)S(1)} %get-tuple-element.9) | data formatting | bytes 6144
Async XLA Ops:
  0.6 1.4 %copy-start = (bf16[5,384,384]{2,1,0:T(8,128)(2,1)S(1)}, bf16[5,384,384]{2,1,0:T(8,128)(2,1)}, u32[]{:S(2)}) copy-start(bf16[5,384,384]{2,1,0:T(8,128)(2,1)} %w_row_hbm.1) | copy-start | bytes 4423684
  2.0 1.4 %copy-start.1 = (bf16[5,384,384]{2,1,0:T(8,128)(2,1)S(1)}, bf16[5,384,384]{2,1,0:T(8,128)(2,1)}, u32[]{:S(2)}) copy-start(bf16[5,384,384]{2,1,0:T(8,128)(2,1)} %w_col_hbm.1) | copy-start | bytes 4423684
  3.4 0.9 %copy-start.2 = (bf16[1,384,256]{2,1,0:T(8,128)(2,1)S(1)}, bf16[1,384,256]{2,1,0:T(8,128)(2,1)}, u32[]{:S(2)}) copy-start(bf16[1,384,256]{2,1,0:T(8,128)(2,1)} %param.8) | copy-start | bytes 589828
  4.3 0.9 %copy-start.3 = (bf16[1,384,256]{2,1,0:T(8,128)(2,1)S(1)}, bf16[1,384,256]{2,1,0:T(8,128)(2,1)}, u32[]{:S(2)}) copy-start(bf16[1,384,256]{2,1,0:T(8,128)(2,1)} %param.9) | copy-start | bytes 589828
  5.2 0.9 %copy-start.4 = (bf16[1,384,128]{2,1,0:T(8,128)(2,1)S(1)}, bf16[1,384,128]{2,1,0:T(8,128)(2,1)}, u32[]{:S(2)}) copy-start(bf16[1,384,128]{2,1,0:T(8,128)(2,1)} %param.10) | copy-start | bytes 294916
  6.1 0.9 %copy-start.5 = (bf16[1,384,128]{2,1,0:T(8,128)(2,1)S(1)}, bf16[1,384,128]{2,1,0:T(8,128)(2,1)}, u32[]{:S(2)}) copy-start(bf16[1,384,128]{2,1,0:T(8,128)(2,1)} %param.11) | copy-start | bytes 294916
  7.0 0.7 %copy-start.6 = (s32[2,1,384]{2,1,0:T(1,128)S(1)}, s32[2,1,384]{2,1,0:T(1,128)}, u32[]{:S(2)}) copy-start(s32[2,1,384]{2,1,0:T(1,128)} %offsets.1) | copy-start | bytes 9220
  7.7 0.7 %copy-start.7 = (f32[3,128]{1,0:T(4,128)S(1)}, f32[3,128]{1,0:T(4,128)}, u32[]{:S(2)}) copy-start(f32[3,128]{1,0:T(4,128)} %w_motion.1) | copy-start | bytes 4612

commit v2 on v1

--- a/solution.py
+++ b/solution.py
@@ -234,22 +234,32 @@
     return jnp.concatenate([tall[k * step : k * step + count] for k in range(5)], axis=1)
 
 
+def gate(x):
+    return 0.5 * jnp.tanh(0.5 * x) + 0.5
+
+
 def tap_weights(w_ref, first, low, high):
     return w_ref[:, first : first + 128, low:high].reshape(5 * 128, high - low)
 
 
 def fused_kernel(
     bands,
+    frame1_hbm,
+    frame2_hbm,
+    context_hbm,
+    hidden_init_hbm,
+    offsets_hbm,
+    w_motion_hbm,
+    w_row_hbm,
+    w_col_hbm,
+    hidden_out,
+    flow_out,
     frame1,
     frame2,
     context,
     hidden_init,
     offsets,
     w_motion,
-    w_row_hbm,
-    w_col_hbm,
-    hidden_out,
-    flow_out,
     w_row,
     w_col,
     strips,
@@ -274,7 +284,7 @@
     gate_row,
     acc_col,
     acc_row2,
-    w_sem,
+    load_sem,
     strip_send,
     strip_recv,
     ctx_ssem,
@@ -293,10 +303,23 @@
     me = lax.axis_index("band")
     pair = lax.axis_index("pair")
 
-    copy_row = pltpu.make_async_copy(w_row_hbm, w_row, w_sem.at[0])
-    copy_col = pltpu.make_async_copy(w_col_hbm, w_col, w_sem.at[1])
-    copy_row.start()
-    copy_col.start()
+    loads = [
+        pltpu.make_async_copy(source, target, load_sem.at[i])
+        for i, (source, target) in enumerate(
+            (
+                (frame2_hbm, frame2),
+                (context_hbm, context),
+                (hidden_init_hbm, hidden_init),
+                (w_row_hbm, w_row),
+                (frame1_hbm, frame1),
+                (offsets_hbm, offsets),
+                (w_motion_hbm, w_motion),
+                (w_col_hbm, w_col),
+            )
+        )
+    ]
+    for load in loads:
+        load.start()
 
     barrier = pltpu.get_barrier_semaphore()
 
@@ -308,6 +331,7 @@
 
     lax.fori_loop(1, bands, greet, 0)
 
+    loads[0].wait()
     blocks = frame2[...].astype(F32).reshape(grid_cols, 8, frame2.shape[1])
     strips[pl.ds(me, 1)] = (jnp.sum(blocks, axis=1) / 2.0).astype(BF)[None]
 
@@ -320,6 +344,8 @@
     for ref in (win_ctx, win_mot, win_hid, win_gate):
         zero_ends(ref, bands * win)
 
+    loads[1].wait()
+    loads[2].wait()
     pad_ctx[8 : 8 + width, :] = context[...].astype(F32)
     pad_hid[8 : 8 + width, :] = hidden_init[...].astype(F32)
 
@@ -330,45 +356,39 @@
 
     stage_windows(ctx_stage, pad_ctx)
 
-    def send(stage, recv, ssem, rsem, to):
-        return pltpu.make_async_remote_copy(
-            src_ref=stage.at[to],
-            dst_ref=recv.at[me],
-            send_sem=ssem.at[to],
-            recv_sem=rsem.at[me],
-            device_id=(to, pair),
-            device_id_type=MESH,
-        )
+    order = sorted(range(1, bands), key=lambda k: abs(2 * k - bands))
 
     def scatter(stage, recv, ssem, rsem):
-        def one(k, carry):
-            send(stage, recv, ssem, rsem, lax.rem(me + k, bands)).start()
+        for k in order:
+            to = lax.rem(me + k, bands)
+            pltpu.make_async_remote_copy(
+                src_ref=stage.at[to],
+                dst_ref=recv.at[me],
+                send_sem=ssem,
+                recv_sem=rsem,
+                device_id=(to, pair),
+                device_id_type=MESH,
+            ).start()
+
+    def wait_bytes(ref, sem):
+        most = ref.at[pl.ds(0, bands - 1)]
+        pltpu.make_async_copy(most, most, sem).wait()
+
+    def collect(stage, recv, rsem):
+        wait_bytes(recv, rsem)
+        half = stage.shape[1] // 2 if stage.shape[1] == win else 0
+
+        def keep(i, carry):
+            recv[pl.ds(me, 1), pl.ds(i * half, half)] = stage[pl.ds(me, 1), pl.ds(i * half, half)]
             return carry
 
-        lax.fori_loop(1, bands, one, 0)
-        recv[pl.ds(me, 1)] = stage[pl.ds(me, 1)]
-
-    def collect(stage, recv, ssem, rsem):
-        def one(k, carry):
-            source = lax.rem(me + bands - k, bands)
-            pltpu.make_async_remote_copy(
-                src_ref=stage.at[source],
-                dst_ref=recv.at[source],
-                send_sem=ssem.at[source],
-                recv_sem=rsem.at[source],
-                device_id=(source, pair),
-                device_id_type=MESH,
-            ).wait_recv()
-            return carry
-
-        lax.fori_loop(1, bands, one, 0)
-
-    def sent(stage, recv, ssem, rsem):
-        def one(k, carry):
-            send(stage, recv, ssem, rsem, lax.rem(me + k, bands)).wait_send()
-            return carry
-
-        lax.fori_loop(1, bands, one, 0)
+        if half:
+            lax.fori_loop(0, 2, keep, 0)
+        else:
+            recv[pl.ds(me, 1)] = stage[pl.ds(me, 1)]
+
+    def sent(stage, ssem):
+        wait_bytes(stage, ssem)
 
     pl.semaphore_wait(barrier, bands - 1)
 
@@ -415,14 +435,13 @@
     pass_on(me, line[3], 3)
     pass_on(me, sibling, 4)
 
-    copy_row.wait()
+    loads[3].wait()
     gate_row[...] = mm(shifted_taps(pad_hid, width), tap_weights(w_row, 0, 0, 256))
 
     for i in (1, 2, 3):
         arrived(line[i])
         pass_on(line[i], across, 4 + i)
         pass_on(line[i], sibling, 7 + i)
-    scatter(ctx_stage, ctx_recv, ctx_ssem, ctx_rsem)
     acc_row[...] = mm(shifted_taps(pad_ctx, width), tap_weights(w_row, 128, 0, 384))
     for i in (0, 1, 2, 3):
         arrived(across_line[i])
@@ -432,6 +451,9 @@
     for i in (0, 1, 2, 3):
         arrived(across_line[i] + 1 - 2 * core)
 
+    scatter(ctx_stage, ctx_recv, ctx_ssem, ctx_rsem)
+    for load in loads[4:7]:
+        load.wait()
     scores[...] = lax.dot_general(
         strips[...].reshape(bands * grid_cols, frame1.shape[1]),
         frame1[...],
@@ -514,8 +536,8 @@
         )
     acc = mm(shifted_taps(pad_mot, width), tap_weights(w_row, 256, 0, 384)) + acc_row[...]
     start = pad_hid[8 : 8 + width, :]
-    update = jax.nn.sigmoid(gate_row[:, 0:128] + acc[:, 0:128])
-    reset = jax.nn.sigmoid(gate_row[:, 128:256] + acc[:, 128:256])
+    update = gate(gate_row[:, 0:128] + acc[:, 0:128])
+    reset = gate(gate_row[:, 128:256] + acc[:, 128:256])
     pad_gate[8 : 8 + width, :] = reset * start
     candidate = jnp.tanh(
         mm(shifted_taps(pad_gate, width), tap_weights(w_row, 0, 256, 384)) + acc[:, 256:384]
@@ -525,13 +547,13 @@
     scatter(hid_stage, hid_recv, hid_ssem, hid_rsem)
 
     pixels = bands * win
-    collect(ctx_stage, ctx_recv, ctx_ssem, ctx_rsem)
-    copy_col.wait()
+    collect(ctx_stage, ctx_recv, ctx_rsem)
+    loads[7].wait()
     ctx = ctx_recv[...].reshape(pixels, 128)
     win_ctx[8 : 8 + pixels, :] = ctx.astype(F32)
     acc_col[...] = mm(row_taps(ctx, win), tap_weights(w_col, 128, 0, 384))
     acc_row2[...] = mm(shifted_taps(win_ctx, pixels), tap_weights(w_row, 128, 0, 384))
-    collect(flow_stage, flow_recv, flow_ssem, flow_rsem)
+    collect(flow_stage, flow_recv, flow_rsem)
     upright = jnp.concatenate(
         [flow_recv[r] for r in range(bands)] + [jnp.zeros((128 - bands, 128), F32)], axis=0
     ).T
@@ -545,14 +567,14 @@
     acc_col[...] += mm(row_taps(motion, win), tap_weights(w_col, 256, 0, 384))
     acc_row2[...] += mm(shifted_taps(win_mot, pixels), tap_weights(w_row, 256, 0, 384))
 
-    collect(hid_stage, hid_recv, hid_ssem, hid_rsem)
+    collect(hid_stage, hid_recv, hid_rsem)
     state_half = hid_recv[...].reshape(pixels, 128)
     state = state_half.astype(F32)
 
     def gru(state, half, acc, weight, taps_of):
         pre = mm(taps_of(half, win_hid), tap_weights(weight, 0, 0, 256)) + acc[:, 0:256]
-        update = jax.nn.sigmoid(pre[:, 0:128])
-        reset = jax.nn.sigmoid(pre[:, 128:256])
+        update = gate(pre[:, 0:128])
+        reset = gate(pre[:, 128:256])
         gated = (reset * half.astype(F32)).astype(BF)
         candidate = jnp.tanh(
             mm(taps_of(gated, win_gate), tap_weights(weight, 0, 256, 384)) + acc[:, 256:384]
@@ -576,12 +598,12 @@
     scatter(out_stage, out_recv, out_ssem, out_rsem)
     for copy in started:
         copy.wait_send()
-    sent(ctx_stage, ctx_recv, ctx_ssem, ctx_rsem)
-    sent(flow_stage, flow_recv, flow_ssem, flow_rsem)
-    sent(hid_stage, hid_recv, hid_ssem, hid_rsem)
-    collect(out_stage, out_recv, out_ssem, out_rsem)
+    sent(ctx_stage, ctx_ssem)
+    sent(flow_stage, flow_ssem)
+    sent(hid_stage, hid_ssem)
+    collect(out_stage, out_recv, out_rsem)
     hidden_out[...] = out_recv[...]
-    sent(out_stage, out_recv, out_ssem, out_rsem)
+    sent(out_stage, out_ssem)
 
 
 def per_device_columns(
@@ -592,7 +614,7 @@
     win = own + 2 * HALO
     pixels = bands * win
     vmem = pl.BlockSpec(memory_space=pltpu.VMEM)
-    hbm = pl.BlockSpec(memory_space=pl.ANY)
+    hbm = pl.BlockSpec(memory_space=pltpu.HBM)
     dma = pltpu.SemaphoreType.DMA
     tall = pltpu.VMEM((width + 16, 128), F32)
     wide = pltpu.VMEM((pixels + 16, 128), F32)
@@ -602,9 +624,15 @@
             jax.ShapeDtypeStruct((bands, own, 128), BF),
             jax.ShapeDtypeStruct((2, 1, width), F32),
         ),
-        in_specs=[vmem] * 6 + [hbm] * 2,
+        in_specs=[hbm] * 8,
         out_specs=(vmem, vmem),
         scratch_shapes=[
+            pltpu.VMEM((width, channels), BF),
+            pltpu.VMEM((width, channels), BF),
+            pltpu.VMEM((width, 128), BF),
+            pltpu.VMEM((width, 128), BF),
+            pltpu.VMEM(offsets.shape, jnp.int32),
+            pltpu.VMEM(w_motion.shape, F32),
             pltpu.VMEM(w_row.shape, BF),
             pltpu.VMEM(w_col.shape, BF),
             pltpu.VMEM((bands, width // 8, channels), BF),
@@ -629,12 +657,13 @@
             pltpu.VMEM((width, 256), F32),
             pltpu.VMEM((pixels, 384), F32),
             pltpu.VMEM((pixels, 384), F32),
-            dma((2,)),
+            dma((8,)),
             dma((15,)),
+            dma((bands,)),
         ]
-        + [dma((bands,))] * 9,
+        + [dma] * 8,
         compiler_params=pltpu.CompilerParams(
-            collective_id=0, has_side_effects=True, vmem_limit_bytes=48 * 1024 * 1024
+            collective_id=0, has_side_effects=True, vmem_limit_bytes=63 * 1024 * 1024
         ),
         cost_estimate=pl.CostEstimate(
             flops=2_400_000_000, bytes_accessed=4_500_000, transcendentals=700_000

time: 40 us -> 32.9 us (0.82)
  local copies, waits for them, and re-layouts: 8.32 us -> 1.26 us
  other arithmetic: 0.69 us -> 1.58 us
  Pallas kernels: 30 us -> 29.2 us
    unnamed x17 -> x1, local copies, waits for them, and re-layouts: 8.32 us -> 1.26 us
    reshape x1, other arithmetic: 0.69 us -> 1.58 us  [per_device_columns(): return (hidden.astype(F32).reshape(1, width, 128), flow)]
    pallas_call x1, Pallas kernels: 30 us -> 29.2 us  [per_device_columns(): pl.pallas_call(functools.partial(fused_kernel, bands), out_shape=(jax.Sha...]
where the time goes in v2:
time: 32.9 us; the launch traced here: 32.7 us
  Pallas kernels  29.2 us (89%)
  other arithmetic  1.58 us (5%)
  local copies, waits for them, and re-layouts  1.26 us (4%)
  between operations  0.64 us (2%)
    pallas_call x1, Pallas kernels, per_device_columns(): pl.pallas_call(functools.partial(fused_kernel, bands), out_shape=(jax.Sha...  29.2 us
    reshape x1, other arithmetic, per_device_columns(): return (hidden.astype(F32).reshape(1, width, 128), flow)  1.58 us
    unnamed x1, local copies, waits for them, and re-layouts  1.26 us

profile of v2, /device:TPU:0, one launch (start us, length us, event | category | flops | bytes accessed | tf_op | source)
XLA Modules:
  0.0 32.7 jit_solution(11061624350919291217)
XLA Ops:
  0.6 29.2 %shard_map.95 = (bf16[16,24,128]{2,1,0:T(8,128)(2,1)}, f32[2,1,384]{2,1,0:T(1,128)}) custom-call(bf16[384,256]{1,0:T(8,128)(2,1)} %bitcast.9, bf16[384,256]{1,0:T(8,128)(2,1)} %bitcast.10, bf16[384,128]{1,0:T(8,128)(2,1)} %bitcast.11, bf16[384,128]{1,0:T(8,128)(2,1)} %bitcast.12, s32[2,1,384]{2,1,0:T(1,128)} %offsets_hbm.1, f32[3,128]{1,0:T(4,128)} %w_motion_hbm.1, ...), custom_call_target="tpu_custom_call" | custom-call | flops 2400000000 | bytes 4500000 | tf_op jit(solution)/shard_map/pallas_call | solution.py:621
  29.9 1.6 %bitcast_convert_fusion = f32[1,384,128]{2,1,0:T(8,128)} fusion(bf16[1,384,128]{2,1,0:T(8,128)(2,1)} %bitcast.8), kind=kLoop, calls=%fused_computation | loop fusion | flops 49152 | bytes 294912 | tf_op jit(solution)/shard_map/reshape | solution.py:681
  31.4 1.3 %copy.11 = f32[2,1,384]{2,1,0:T(1,128)} copy(f32[2,1,384]{2,1,0:T(1,128)} %get-tuple-element.9) | data formatting | bytes 6144

commit v3 on v2

--- a/solution.py
+++ b/solution.py
@@ -429,8 +429,8 @@
             device_id_type=MESH,
         ).wait_recv()
 
+    pass_on(me, across, 1)
     pass_on(me, line[1], 0)
-    pass_on(me, across, 1)
     pass_on(me, line[2], 2)
     pass_on(me, line[3], 3)
     pass_on(me, sibling, 4)
@@ -446,14 +446,14 @@
     for i in (0, 1, 2, 3):
         arrived(across_line[i])
         pass_on(across_line[i], sibling, 11 + i)
+    scatter(ctx_stage, ctx_recv, ctx_ssem, ctx_rsem)
+    for load in loads[4:7]:
+        load.wait()
     for i in (0, 1, 2, 3):
         arrived(line[i] + 1 - 2 * core)
     for i in (0, 1, 2, 3):
         arrived(across_line[i] + 1 - 2 * core)
 
-    scatter(ctx_stage, ctx_recv, ctx_ssem, ctx_rsem)
-    for load in loads[4:7]:
-        load.wait()
     scores[...] = lax.dot_general(
         strips[...].reshape(bands * grid_cols, frame1.shape[1]),
         frame1[...],

time: 32.9 us -> 32.6 us (level)
  no operation moved by 1% of the time
where the time goes in v3:
time: 32.6 us; the launch traced here: 32.4 us
  Pallas kernels  28.9 us (89%)
  other arithmetic  1.58 us (5%)
  local copies, waits for them, and re-layouts  1.26 us (4%)
  between operations  0.64 us (2%)
    pallas_call x1, Pallas kernels, per_device_columns(): pl.pallas_call(functools.partial(fused_kernel, bands), out_shape=(jax.Sha...  28.9 us
    reshape x1, other arithmetic, per_device_columns(): return (hidden.astype(F32).reshape(1, width, 128), flow)  1.58 us
    unnamed x1, local copies, waits for them, and re-layouts  1.26 us

profile of v3, /device:TPU:0, one launch (start us, length us, event | category | flops | bytes accessed | tf_op | source)
XLA Modules:
  0.0 32.4 jit_solution(15105947882302040065)
XLA Ops:
  0.6 28.9 %shard_map.95 = (bf16[16,24,128]{2,1,0:T(8,128)(2,1)}, f32[2,1,384]{2,1,0:T(1,128)}) custom-call(bf16[384,256]{1,0:T(8,128)(2,1)} %bitcast.9, bf16[384,256]{1,0:T(8,128)(2,1)} %bitcast.10, bf16[384,128]{1,0:T(8,128)(2,1)} %bitcast.11, bf16[384,128]{1,0:T(8,128)(2,1)} %bitcast.12, s32[2,1,384]{2,1,0:T(1,128)} %offsets_hbm.1, f32[3,128]{1,0:T(4,128)} %w_motion_hbm.1, ...), custom_call_target="tpu_custom_call" | custom-call | flops 2400000000 | bytes 4500000 | tf_op jit(solution)/shard_map/pallas_call | solution.py:621
  29.6 1.6 %bitcast_convert_fusion = f32[1,384,128]{2,1,0:T(8,128)} fusion(bf16[1,384,128]{2,1,0:T(8,128)(2,1)} %bitcast.8), kind=kLoop, calls=%fused_computation | loop fusion | flops 49152 | bytes 294912 | tf_op jit(solution)/shard_map/reshape | solution.py:681
  31.2 1.3 %copy.11 = f32[2,1,384]{2,1,0:T(1,128)} copy(f32[2,1,384]{2,1,0:T(1,128)} %get-tuple-element.9) | data formatting | bytes 6144

commit v4 on v3

--- a/solution.py
+++ b/solution.py
@@ -551,8 +551,8 @@
     loads[7].wait()
     ctx = ctx_recv[...].reshape(pixels, 128)
     win_ctx[8 : 8 + pixels, :] = ctx.astype(F32)
-    acc_col[...] = mm(row_taps(ctx, win), tap_weights(w_col, 128, 0, 384))
-    acc_row2[...] = mm(shifted_taps(win_ctx, pixels), tap_weights(w_row, 128, 0, 384))
+    ctx_down = row_taps(ctx, win)
+    ctx_along = shifted_taps(win_ctx, pixels)
     collect(flow_stage, flow_recv, flow_rsem)
     upright = jnp.concatenate(
         [flow_recv[r] for r in range(bands)] + [jnp.zeros((128 - bands, 128), F32)], axis=0
@@ -564,8 +564,16 @@
             upright[2 * win : 3 * win, r : r + 1],
         )
     motion = win_mot[8 : 8 + pixels, :].astype(BF)
-    acc_col[...] += mm(row_taps(motion, win), tap_weights(w_col, 256, 0, 384))
-    acc_row2[...] += mm(shifted_taps(win_mot, pixels), tap_weights(w_row, 256, 0, 384))
+    for acc_ref, weight, both in (
+        (acc_col, w_col, (ctx_down, row_taps(motion, win))),
+        (acc_row2, w_row, (ctx_along, shifted_taps(win_mot, pixels))),
+    ):
+        acc_ref[...] = mm(
+            jnp.concatenate(both, axis=1),
+            jnp.concatenate(
+                [tap_weights(weight, 128, 0, 384), tap_weights(weight, 256, 0, 384)], axis=0
+            ),
+        )
 
     collect(hid_stage, hid_recv, hid_rsem)
     state_half = hid_recv[...].reshape(pixels, 128)

time: 32.6 us -> 32.7 us (level)
  no operation moved by 1% of the time
where the time goes in v4:
time: 32.7 us; the launch traced here: 32.5 us
  Pallas kernels  29 us (89%)
  other arithmetic  1.58 us (5%)
  local copies, waits for them, and re-layouts  1.26 us (4%)
  between operations  0.64 us (2%)
    pallas_call x1, Pallas kernels, per_device_columns(): pl.pallas_call(functools.partial(fused_kernel, bands), out_shape=(jax.Sha...  29 us
    reshape x1, other arithmetic, per_device_columns(): return (hidden.astype(F32).reshape(1, width, 128), flow)  1.58 us
    unnamed x1, local copies, waits for them, and re-layouts  1.26 us

profile of v4, /device:TPU:0, one launch (start us, length us, event | category | flops | bytes accessed | tf_op | source)
XLA Modules:
  0.0 32.5 jit_solution(4227546273862092054)
XLA Ops:
  0.6 29.0 %shard_map.95 = (bf16[16,24,128]{2,1,0:T(8,128)(2,1)}, f32[2,1,384]{2,1,0:T(1,128)}) custom-call(bf16[384,256]{1,0:T(8,128)(2,1)} %bitcast.9, bf16[384,256]{1,0:T(8,128)(2,1)} %bitcast.10, bf16[384,128]{1,0:T(8,128)(2,1)} %bitcast.11, bf16[384,128]{1,0:T(8,128)(2,1)} %bitcast.12, s32[2,1,384]{2,1,0:T(1,128)} %offsets_hbm.1, f32[3,128]{1,0:T(4,128)} %w_motion_hbm.1, ...), custom_call_target="tpu_custom_call" | custom-call | flops 2400000000 | bytes 4500000 | tf_op jit(solution)/shard_map/pallas_call | solution.py:629
  29.7 1.6 %bitcast_convert_fusion = f32[1,384,128]{2,1,0:T(8,128)} fusion(bf16[1,384,128]{2,1,0:T(8,128)(2,1)} %bitcast.8), kind=kLoop, calls=%fused_computation | loop fusion | flops 49152 | bytes 294912 | tf_op jit(solution)/shard_map/reshape | solution.py:689
  31.3 1.3 %copy.11 = f32[2,1,384]{2,1,0:T(1,128)} copy(f32[2,1,384]{2,1,0:T(1,128)} %get-tuple-element.9) | data formatting | bytes 6144
